TPU v7x, 1024 devices: a whole 4x8x16 slice. The times are simulated.
1024 devices in a mesh: expert: 16 (over y, core), tensor: 16 (over z), dp: 4 (over x).
Axes of the slice: x: 4, y: 8, z: 16, core: 2. Of those that a mesh axis runs over, the one named last changes fastest.
Arguments:
- cotangent: bfloat16 [64, 128, 7168], P(('expert', 'dp'), 'tensor'), may hold values from -6 to 6
- routed_expert_index: int32 [64, 128, 8], P(('expert', 'dp')), may hold values from 0 to 127, all different within a row; in each aligned block of 128 rows (0 to 127, 128 to 255, ..., all dimensions but the last counted through in order) at most 12 rows name the same one
- chosen_gate_weight: float32 [64, 128, 8], P(('expert', 'dp')), may hold values from 0.05 to 0.6
- routed_down_weight: bfloat16 [128, 1024, 7168], P(('expert', 'dp'), None, 'tensor'), may hold values from -0.1875 to 0.1875
- routed_adapter_input_map: bfloat16 [128, 1024, 16], P(('expert', 'dp'), 'tensor'), may hold values from -0.1875 to 0.1875
- routed_adapter_output_map: bfloat16 [128, 16, 7168], P(('expert', 'dp'), None, 'tensor'), may hold values from -0.0625 to 0.0625
- routed_gate_saved: bfloat16 [1024, 128, 768], P('tensor', ('expert', 'dp')), may hold values from -6 to 6
- routed_up_saved: bfloat16 [1024, 128, 768], P('tensor', ('expert', 'dp')), may hold values from -6 to 6
- shared_down_weight: bfloat16 [2048, 7168], P('tensor'), may hold values from -0.125 to 0.125
- shared_adapter_input_map: bfloat16 [2048, 16], P('tensor'), may hold values from -0.125 to 0.125
- shared_adapter_output_map: bfloat16 [16, 7168], replicated, may hold values from -0.0625 to 0.0625
- shared_gate_saved: bfloat16 [64, 128, 2048], P(('expert', 'dp'), None, 'tensor'), may hold values from -6 to 6
- shared_up_saved: bfloat16 [64, 128, 2048], P(('expert', 'dp'), None, 'tensor'), may hold values from -6 to 6
Outputs:
- grad_gate_routed: bfloat16 [1024, 128, 768], P('tensor', ('expert', 'dp'))
- grad_up_routed: bfloat16 [1024, 128, 768], P('tensor', ('expert', 'dp'))
- grad_gate_shared: bfloat16 [64, 128, 2048], P(('expert', 'dp'), None, 'tensor')
- grad_up_shared: bfloat16 [64, 128, 2048], P(('expert', 'dp'), None, 'tensor')
- grad_a_routed: float32 [128, 1024, 16], P(('expert', 'dp'), 'tensor')
- grad_b_routed: float32 [128, 16, 7168], P(('expert', 'dp'), None, 'tensor')
- grad_a_shared: float32 [2048, 16], P('tensor')
- grad_b_shared: float32 [16, 7168], P(None, 'tensor')
Inputs may be any that keep to these rules, and one draw needn't show every extreme that they name: `routed_expert_index`: each token names 8 different experts; within one token group no expert is named by more than 12 tokens, and in some group one expert is named by exactly 12.
All inputs are finite; a program needn't handle non-finite values.
Results may differ from a plain program's by a relative error of at most 0.024.
Values may be sent and summed in bfloat16 or wider, within the bound.
No kernel may reach another device: no remote copies, remote signals or barrier semaphores. Data moves between devices by JAX's collectives and lax.ppermute only.
A program may use at most 64 MiB of HBM per device.

v0:
```python
import jax
import jax.numpy as jnp
from jax import lax
from jax.sharding import PartitionSpec as P

ADAPTER_SCALE = 2.0


def swiglu_parts(gate_value, up_value):
    gate_float = gate_value.astype(jnp.float32)
    up_float = up_value.astype(jnp.float32)
    sigmoid_gate = jax.nn.sigmoid(gate_float)
    activated = gate_float * sigmoid_gate
    hidden_state = (activated * up_float).astype(jnp.bfloat16)
    gate_factor = up_float * sigmoid_gate * (1.0 + gate_float * (1.0 - sigmoid_gate))
    return (hidden_state, gate_factor, activated)


def bucket_targets(group_ids, group_count, expert_local, capacity):
    flattened = group_ids.reshape(-1)
    onehot = (
        flattened[:, None] == lax.iota(jnp.int32, expert_local * group_count)[None, :]
    ).astype(jnp.int32)
    before = jnp.cumsum(onehot, axis=0) - onehot
    slot_index = jnp.sum(before * onehot, axis=1)
    return (
        flattened % expert_local * (group_count * capacity)
        + flattened // expert_local * capacity
        + slot_index
    )


def shards(
    cotangent,
    routed_expert_index,
    chosen_gate_weight,
    routed_down_weight,
    routed_adapter_input_map,
    routed_adapter_output_map,
    routed_gate_saved,
    routed_up_saved,
    shared_down_weight,
    shared_adapter_input_map,
    shared_adapter_output_map,
    shared_gate_saved,
    shared_up_saved,
):
    n_expert_axis = lax.axis_size("expert")
    n_data = lax.axis_size("dp")
    group_count = n_expert_axis * n_data
    expert_local = routed_down_weight.shape[0]
    slice_width = routed_down_weight.shape[2]
    slot_count = routed_gate_saved.shape[2]
    capacity = slot_count // group_count
    weight_scale_factor = ADAPTER_SCALE / group_count
    contract_trailing = (((1,), (1,)), ((), ()))
    contract_first = (((0,), (0,)), ((), ()))
    token_row_block = lax.all_gather(cotangent, "tensor", axis=1, tiled=True)[0]
    token_total = token_row_block.shape[0]
    own_columns = lax.dynamic_slice_in_dim(
        token_row_block, lax.axis_index("tensor") * slice_width, slice_width, 1
    )
    targets = bucket_targets(routed_expert_index[0], group_count, expert_local, capacity).reshape(
        token_total, -1
    )
    bucket_total = expert_local * group_count * capacity
    matches = targets[None, :, :] == lax.iota(jnp.int32, bucket_total)[:, None, None]
    selector = jnp.any(matches, axis=2).astype(jnp.bfloat16)
    bucket_weight = jnp.sum(jnp.where(matches, chosen_gate_weight[0][None, :, :], 0.0), axis=(1, 2))
    selected = jnp.dot(selector, own_columns, preferred_element_type=jnp.float32)
    outgoing = (bucket_weight[:, None] * selected).astype(jnp.bfloat16)
    outgoing = outgoing.reshape(expert_local, group_count, capacity, slice_width)
    arrived = lax.all_to_all(outgoing, ("expert", "dp"), split_axis=1, concat_axis=1, tiled=True)
    routed_output = arrived.reshape(expert_local, slot_count, slice_width)
    shared_gradient = lax.dot_general(
        token_row_block, shared_down_weight, contract_trailing, preferred_element_type=jnp.float32
    )
    shared_rank_output = lax.dot_general(
        token_row_block,
        shared_adapter_output_map,
        contract_trailing,
        preferred_element_type=jnp.float32,
    ).astype(jnp.bfloat16)
    shared_gradient = shared_gradient + ADAPTER_SCALE * lax.dot_general(
        shared_rank_output,
        shared_adapter_input_map,
        contract_trailing,
        preferred_element_type=jnp.float32,
    )
    shared_hidden_state, shared_gate_factor, shared_activated = swiglu_parts(
        shared_gate_saved[0], shared_up_saved[0]
    )
    shared_inner_portion = jnp.dot(
        shared_hidden_state, shared_adapter_input_map, preferred_element_type=jnp.float32
    )
    routed_hidden_state, routed_gate_factor, routed_activated = swiglu_parts(
        routed_gate_saved, routed_up_saved
    )
    routed_inner_part = jnp.einsum(
        "tom,oty->oym",
        routed_hidden_state,
        routed_adapter_input_map,
        preferred_element_type=jnp.float32,
    )
    routed_rank_part = jnp.einsum(
        "bim,btm->bti", routed_output, routed_adapter_output_map, preferred_element_type=jnp.float32
    )
    routed_rank, routed_inner, shared_inner = (
        lax.psum(routed_rank_part.astype(jnp.bfloat16), "tensor").astype(jnp.float32),
        lax.psum(routed_inner_part.astype(jnp.bfloat16), "tensor").astype(jnp.float32),
        lax.psum(shared_inner_portion.astype(jnp.bfloat16), "tensor").astype(jnp.float32),
    )
    hidden_gradient = lax.psum_scatter(
        jnp.einsum(
            "efd,esd->fes", routed_down_weight, routed_output, preferred_element_type=jnp.float32
        ).astype(jnp.bfloat16),
        "tensor",
        scatter_dimension=0,
        tiled=True,
    ).astype(jnp.float32)
    rank_cast_back = routed_rank.astype(jnp.bfloat16)
    hidden_gradient = hidden_gradient + ADAPTER_SCALE * jnp.einsum(
        "wgl,wkg->kwl", rank_cast_back, routed_adapter_input_map, preferred_element_type=jnp.float32
    )
    grad_gate_routed = (hidden_gradient * routed_gate_factor).astype(jnp.bfloat16)
    grad_up_routed = (hidden_gradient * routed_activated).astype(jnp.bfloat16)
    inner_cast_back = routed_inner.astype(jnp.bfloat16)
    grad_a_routed = weight_scale_factor * jnp.einsum(
        "fes,ers->efr", routed_hidden_state, rank_cast_back, preferred_element_type=jnp.float32
    )
    grad_b_routed = weight_scale_factor * jnp.einsum(
        "ers,esd->erd", inner_cast_back, routed_output, preferred_element_type=jnp.float32
    )
    grad_gate_shared = (shared_gradient * shared_gate_factor).astype(jnp.bfloat16)[None]
    grad_up_shared = (shared_gradient * shared_activated).astype(jnp.bfloat16)[None]
    shared_inner_rounded = shared_inner.astype(jnp.bfloat16)
    adapter_a = lax.dot_general(
        shared_hidden_state, shared_rank_output, contract_first, preferred_element_type=jnp.float32
    )
    adapter_b = lax.dot_general(
        shared_inner_rounded, own_columns, contract_first, preferred_element_type=jnp.float32
    )
    adapter_a, adapter_b = lax.psum((adapter_a, adapter_b), ("expert", "dp"))
    grad_a_shared = weight_scale_factor * adapter_a
    grad_b_shared = weight_scale_factor * adapter_b
    return (
        grad_gate_routed,
        grad_up_routed,
        grad_gate_shared,
        grad_up_shared,
        grad_a_routed,
        grad_b_routed,
        grad_a_shared,
        grad_b_shared,
    )


def solution(mesh):
    placed = (
        P(("expert", "dp"), "tensor", None),
        P(("expert", "dp"), None, None),
        P(("expert", "dp"), None, None),
        P(("expert", "dp"), None, "tensor"),
        P(("expert", "dp"), "tensor", None),
        P(("expert", "dp"), None, "tensor"),
        P("tensor", ("expert", "dp"), None),
        P("tensor", ("expert", "dp"), None),
        P("tensor", None),
        P("tensor", None),
        P(),
        P(("expert", "dp"), None, "tensor"),
        P(("expert", "dp"), None, "tensor"),
    )
    return jax.shard_map(
        shards,
        mesh=mesh,
        in_specs=placed,
        out_specs=(
            P("tensor", ("expert", "dp"), None),
            P("tensor", ("expert", "dp"), None),
            P(("expert", "dp"), None, "tensor"),
            P(("expert", "dp"), None, "tensor"),
            P(("expert", "dp"), "tensor", None),
            P(("expert", "dp"), None, "tensor"),
            P("tensor", None),
            P(None, "tensor"),
        ),
        check_vma=False,
    )
```

profile of v0, /device:TPU:1, one launch (start us, length us, event | category | flops | bytes accessed | tf_op | source)
XLA Modules:
  0.0 555.1 jit_solution(4930140015126319271)
XLA Ops:
  7.2 0.0 all-gather.2.cloned.1.call-start
  7.2 0.7 all-gather.2.cloned.1.call-update
  7.9 0.8 copy.70
  8.7 0.1 eq.42
  8.8 0.1 eq.46
  8.9 0.1 copy.76
  9.0 0.2 fusion.18
  9.3 0.1 copy.77
  9.4 0.4 fusion.17
  9.8 0.1 reduce_sum.21
  9.9 0.1 fusion.41
  10.0 5.6 %fusion = pred[1536,128]{1,0:T(8,128)(4,1)S(1)} fusion(s32[128,8]{0,1:T(8,128)S(1)} %copy.78), kind=kLoop, calls=%fused_computation.2 | loop fusion | flops 2949120 | bytes 200704 | tf_op jit(solution)/shard_map/reduce_or | solution.py:68
  15.6 11.5 %select_reduce_fusion = f32[1536]{0:T(1024)S(1)} fusion(f32[128,8]{0,1:T(8,128)S(1)} %bitcast.84, s32[128,8]{0,1:T(8,128)S(1)} %copy.78), kind=kLoop, calls=%fused_computation | loop fusion | flops 4717056 | bytes 14336 | tf_op jit(solution)/shard_map/reduce_sum | solution.py:69
  27.1 59.0 %all-gather.2.cloned.1.call-done = bf16[1,128,7168]{2,1,0:T(8,128)(2,1)} async-done(((bf16[1,8,7168]{2,1,0:T(8,128)(2,1)}), bf16[1,128,7168]{2,1,0:T(8,128)(2,1)}) %all-gather.2.cloned.1.call-update) | async-done | bytes 1835024 | tf_op jit(solution)/shard_map/all_gather | solution.py:58
  86.1 2.7 fusion.1
  88.7 1.7 copy.79
  90.4 1.6 reshape.47
  92.0 4.4 copy.80
  96.4 20.3 %all-to-all-start = ((bf16[2,64,12,448]{3,0,2,1:T(2,128)(2,1)}), bf16[2,64,12,448]{3,0,2,1:T(2,128)(2,1)S(1)}, u32[]{:S(2)}, u32[]{:S(2)}) async-start(bf16[2,64,12,448]{3,0,2,1:T(2,128)(2,1)} %copy.80), calls=%async_computation | async-start | bytes 3145728 | tf_op jit(solution)/shard_map/all_to_all | solution.py:73
  116.7 0.0 all-reduce.8.cloned.1.call-start
  116.8 1.3 fusion.23
  118.1 0.7 copy-done.3
  118.8 0.8 fusion.12
  119.5 2.1 fusion.13
  121.6 0.2 convolution_multiply_fusion.3
  121.8 2.8 fusion.51
  124.6 0.7 convolution_convert_fusion.2
  125.4 30.0 %all-to-all-done = bf16[2,64,12,448]{3,0,2,1:T(2,128)(2,1)S(1)} async-done(((bf16[2,64,12,448]{3,0,2,1:T(2,128)(2,1)}), bf16[2,64,12,448]{3,0,2,1:T(2,128)(2,1)S(1)}, u32[]{:S(2)}, u32[]{:S(2)}) %all-to-all-start) | async-done | bytes 1376288 | tf_op jit(solution)/shard_map/all_to_all | solution.py:73
  155.4 1.2 copy-done.2
  156.6 3.7 copy.81
  160.3 0.9 fusion.11
  161.2 0.0 all-reduce.8.cloned.1.call-update
  161.2 0.0 all-reduce.6.cloned.1.call-start
  161.3 3.5 convert_bitcast_fusion
  164.8 8.7 %copy.82 = bf16[1024,2,768]{2,1,0:T(2,128)(2,1)} copy(bf16[1024,2,768]{0,2,1:T(8,128)(2,1)} %convert_bitcast_fusion) | data formatting | bytes 6291456 | tf_op jit(solution)/shard_map/convert_element_type | solution.py:116
  173.5 1.3 dynamic-slice.1
  175.5 0.1 fusion.57
  175.7 109.7 %all-reduce.8.cloned.1.call-done = (bf16[2,16,768]{2,1,0:T(8,128)(2,1)}, bf16[2,16,768]{2,1,0:T(8,128)(2,1)}, bf16[128,16]{0,1:T(8,128)(2,1)}) async-done(((bf16[2,16,768]{2,1,0:T(8,128)(2,1)}, bf16[2,16,768]{2,1,0:T(8,128)(2,1)}, bf16[128,16]{0,1:T(8,128)(2,1)}), (bf16[2,16,768]{2,1,0:T(8,128)(2,1)}, bf16[2,16,768]{2,1,0:T(8,128)(2,1)}, bf16[128,16]{0,1:T(8,128)(2,1)})) %all-reduce.8.cloned.1.call-update) | async-done | bytes 102416 | tf_op jit(solution)/shard_map/psum | solution.py:109
  285.4 1.1 fusion.29
  286.5 253.2 %all-reduce.1 = (f32[128,16]{0,1:T(8,128)S(1)}, f32[16,448]{1,0:T(8,128)S(1)}) all-reduce(f32[128,16]{0,1:T(8,128)S(1)} %fusion.57, f32[16,448]{1,0:T(8,128)S(1)} %fusion.29), channel_id=1, replica_groups=mesh['expert'=16,'tensor'=16,'dp'=4] {'expert','dp'}, use_global_device_ids=true, to_apply=%region_8.9 | all-reduce | flops 9216 | bytes 73728 | tf_op jit(solution)/shard_map/psum | solution.py:143
  539.7 0.6 broadcast_multiply_fusion.1
  540.3 0.6 broadcast_multiply_fusion
  540.9 1.6 convolution_multiply_fusion.4
  542.5 1.9 convolution_multiply_fusion.2
  544.4 1.1 constant_dynamic-slice_fusion
  545.5 1.3 multiply_convert_fusion
  546.8 0.9 copy.89
  547.7 0.9 copy.88
  (31 shorter events, 0.2 us)
Async XLA Ops:
  7.2 154.1 %copy-start = (bf16[2,1024,448]{1,2,0:T(8,128)(2,1)S(1)}, bf16[2,1024,448]{1,2,0:T(8,128)(2,1)}, u32[]{:S(2)}) copy-start(bf16[2,1024,448]{1,2,0:T(8,128)(2,1)} %param.16) | copy-start | bytes 5505028
  7.2 78.9 %all-gather.2.cloned.1.call-start = ((), (), s32[]{:S(2)}) async-start(), calls=%async_computation.1 | async-start | bytes 1949696 | tf_op jit(solution)/shard_map/all_gather | solution.py:58
  9.0 6.6 %copy-start.12 = (f32[1,128,8]{1,2,0:T(8,128)S(1)}, f32[1,128,8]{1,2,0:T(8,128)}, u32[]{:S(2)}) copy-start(f32[1,128,8]{1,2,0:T(8,128)} %param.15) | copy-start | bytes 12292
  96.4 22.4 %copy-start.11 = (bf16[2,64,16]{1,2,0:T(8,128)(2,1)S(1)}, bf16[2,64,16]{1,2,0:T(8,128)(2,1)}, u32[]{:S(2)}) copy-start(bf16[2,64,16]{1,2,0:T(8,128)(2,1)} %param.17) | copy-start | bytes 12292
  96.4 59.0 %all-to-all-start = ((bf16[2,64,12,448]{3,0,2,1:T(2,128)(2,1)}), bf16[2,64,12,448]{3,0,2,1:T(2,128)(2,1)S(1)}, u32[]{:S(2)}, u32[]{:S(2)}) async-start(bf16[2,64,12,448]{3,0,2,1:T(2,128)(2,1)} %copy.80), calls=%async_computation | async-start | bytes 3145728 | tf_op jit(solution)/shard_map/all_to_all | solution.py:73
  116.7 4.9 copy-start.10
  116.7 5.1 copy-start.7
  116.7 5.1 copy-start.8
  116.7 168.6 %all-reduce.8.cloned.1.call-start = ((), (), s32[]{:S(2)}) async-start(), calls=%async_computation.3 | async-start | bytes 204800 | tf_op jit(solution)/shard_map/psum | solution.py:109
  116.8 5.1 copy-start.1
  118.1 0.7 copy-start.3
  124.6 35.6 %copy-start.9 = (bf16[2,16,448]{2,1,0:T(8,128)(2,1)S(1)}, bf16[2,16,448]{2,1,0:T(8,128)(2,1)}, u32[]{:S(2)}) copy-start(bf16[2,16,448]{2,1,0:T(8,128)(2,1)} %param.18) | copy-start | bytes 86020
  155.4 1.2 copy-start.2
  161.2 383.2 %all-reduce.6.cloned.1.call-start = ((), (), s32[]{:S(2)}) async-start(), calls=%async_computation.2 | async-start | bytes 6291456
  173.5 367.4 %copy-start.4 = (bf16[64,2,768]{2,0,1:T(8,128)(2,1)S(1)}, bf16[64,2,768]{2,0,1:T(8,128)(2,1)}, u32[]{:S(2)}) copy-start(bf16[64,2,768]{2,0,1:T(8,128)(2,1)} %copy-done.3) | copy-start | bytes 589828
  285.4 260.1 %copy-start.6 = (bf16[2,16,768]{2,1,0:T(8,128)(2,1)S(1)}, bf16[2,16,768]{2,1,0:T(8,128)(2,1)}, u32[]{:S(2)}) copy-start(bf16[2,16,768]{2,1,0:T(8,128)(2,1)} %get-tuple-element.42) | copy-start | bytes 147460
  542.5 3.0 copy-start.5
Sparse Core Ops, SparseCore 0:
  10.7 75.3 all-gather.1
  161.3 123.9 all-reduce.7
  287.9 154.8 all-reduce.5
where the time goes:
time: 559 us; the launch traced here: 555 us
  blocking collectives  253 us (45%)
  waiting for transfers between devices  199 us (36%)
  local copies, waits for them, and re-layouts  27.4 us (5%)
  starting transfers between devices  20.4 us (4%)
  other arithmetic  20.3 us (4%)
  matrix products  19.7 us (4%)
  between operations  14.6 us (3%)
    psum x1, blocking collectives, shards(): adapter_a, adapter_b = lax.psum((adapter_a, adapter_b), ('expert', 'dp'))  253 us
    psum x1, waiting for transfers between devices, shards(): lax.psum(routed_rank_part.astype(jnp.bfloat16), 'tensor')  110 us
    all_gather x1, waiting for transfers between devices, shards(): token_row_block = lax.all_gather(cotangent, 'tensor', axis=1, tiled=True)[0]  59 us
    all_to_all x1, waiting for transfers between devices, shards(): lax.all_to_all(outgoing, ('expert', 'dp'), split_axis=1, concat_axis=1, t...  30 us
    all_to_all x1, starting transfers between devices, shards(): lax.all_to_all(outgoing, ('expert', 'dp'), split_axis=1, concat_axis=1, t...  20.3 us
    reduce_sum x1, other arithmetic, shards(): jnp.sum(jnp.where(matches, chosen_gate_weight[0][None, :, :], 0.0), axis=...  11.5 us
  transfers between devices with their start and end apart: 4, of which 3 were waited for; matrix products, arithmetic and copies ran while one was open for 8% of the time, Pallas kernels for 0%

commit v1 on v0

v1 whole, which is shorter than its diff:
```python
import jax
import jax.numpy as jnp
from jax import lax
from jax.experimental import pallas as pl
from jax.experimental.pallas import tpu as pltpu
from jax.sharding import PartitionSpec as P

ADAPTER_SCALE = 2.0
F32 = jnp.float32
BF16 = jnp.bfloat16
LANES = 128
CHUNK_LO = 512
CHUNK_HI = 640
PACKED = 768


def swiglu_parts(gate_value, up_value):
    gate_float = gate_value.astype(F32)
    up_float = up_value.astype(F32)
    sigmoid_gate = jax.nn.sigmoid(gate_float)
    activated = gate_float * sigmoid_gate
    hidden_state = (activated * up_float).astype(BF16)
    gate_factor = up_float * sigmoid_gate * (1.0 + gate_float * (1.0 - sigmoid_gate))
    return (hidden_state, gate_factor, activated)


def whole(count):
    return [pl.BlockSpec(memory_space=pltpu.VMEM)] * count


def pack_kernel(cot_ref, routed_ref, shared_ref, out_ref):
    n_tensor = out_ref.shape[0] // 8
    width = cot_ref.shape[1] // n_tensor
    per_expert = routed_ref.shape[2] // LANES
    experts = routed_ref.shape[0]
    cot = cot_ref[...].astype(F32)

    def chunk(t):
        if t < experts * per_expert:
            column = t % per_expert * LANES
            return routed_ref[t // per_expert, :, column : column + LANES].astype(F32)
        if t == experts * per_expert:
            return shared_ref[...].astype(F32)
        return jnp.zeros((16, LANES), F32)

    for pair in range(n_tensor // 2):
        even, odd = 2 * pair, 2 * pair + 1
        rows = pl.ds(16 * pair, 16)
        tokens = jnp.concatenate(
            [cot[:, even * width : (even + 1) * width], cot[:, odd * width : (odd + 1) * width]],
            axis=0,
        )
        out_ref[rows, 0:width] = tokens.astype(BF16)
        out_ref[rows, width:CHUNK_LO] = jnp.zeros((16, CHUNK_LO - width), BF16)
        first, second = chunk(even), chunk(odd)
        out_ref[rows, CHUNK_LO:CHUNK_HI] = jnp.concatenate([first[0:8], second[0:8]], 0).astype(BF16)
        out_ref[rows, CHUNK_HI:PACKED] = jnp.concatenate([first[8:16], second[8:16]], 0).astype(BF16)


def dispatch_kernel(index_ref, weight_ref, packed_ref, out_ref, columns_ref, chunk_ref):
    tokens = packed_ref.shape[0]
    width = out_ref.shape[1]
    top = index_ref.shape[0]
    peers = out_ref.shape[0] // 24
    columns = packed_ref[:, 0:width]
    columns_ref[...] = columns
    for half, lane in enumerate((CHUNK_LO, CHUNK_HI)):
        partial = packed_ref[:, lane : lane + LANES].astype(F32).reshape(tokens // 8, 8, LANES)
        chunk_ref[8 * half : 8 * half + 8, :] = jnp.sum(partial, axis=0)
    before = (
        lax.broadcasted_iota(jnp.int32, (tokens, tokens), 0)
        < lax.broadcasted_iota(jnp.int32, (tokens, tokens), 1)
    ).astype(BF16)
    weights, slots = [], []
    for local in range(2):
        expert = 2 * lax.broadcasted_iota(jnp.int32, (peers, tokens), 0) + local
        weight = jnp.zeros((peers, tokens), F32)
        named = jnp.zeros((peers, tokens), F32)
        for k in range(top):
            match = expert == index_ref[k : k + 1, :]
            weight = jnp.where(match, weight_ref[k : k + 1, :], weight)
            named = jnp.where(match, 1.0, named)
        slot = jnp.dot(named.astype(BF16), before, preferred_element_type=F32)
        weights.append(weight)
        slots.append(slot)
    row = lax.broadcasted_iota(jnp.int32, (peers, 24, tokens), 1)
    first = row < 12
    wanted = jnp.where(first, row, row - 12).astype(F32)
    shape = (peers, 24, tokens)
    slot = jnp.where(
        first,
        jnp.broadcast_to(slots[0][:, None, :], shape),
        jnp.broadcast_to(slots[1][:, None, :], shape),
    )
    weight = jnp.where(
        first,
        jnp.broadcast_to(weights[0][:, None, :], shape),
        jnp.broadcast_to(weights[1][:, None, :], shape),
    )
    selector = jnp.where(slot == wanted, weight, 0.0).reshape(peers * 24, tokens)
    high = selector.astype(BF16)
    low = (selector - high.astype(F32)).astype(BF16)
    left = jnp.concatenate([high, low], axis=1)
    right = jnp.concatenate([columns, columns], axis=0)
    out_ref[...] = jnp.dot(left, right, preferred_element_type=F32).astype(BF16)


def routed_kernel(arrived_ref, weight_ref, map_ref, chunk_ref, part_ref, rows_ref, gather_ref, held):
    local, step = pl.program_id(0), pl.program_id(1)
    slots = rows_ref.shape[1]
    block = 192

    @pl.when(step == 0)
    def _():
        i = lax.broadcasted_iota(jnp.int32, (block, 2 * block), 0)
        j = lax.broadcasted_iota(jnp.int32, (block, 2 * block), 1)
        group = lax.shift_right_logical(i * 5462, 16)
        pick = (j - i == 12 * (group + local)).astype(BF16)
        for b in range(slots // block):
            rows = jnp.dot(
                pick,
                arrived_ref[2 * block * b : 2 * block * (b + 1), :],
                preferred_element_type=F32,
            ).astype(BF16)
            held[block * b : block * (b + 1), :] = rows
        rows_ref[0] = held[...]
        rank = lax.dot_general(
            map_ref[0], held[...], (((1,), (1,)), ((), ())), preferred_element_type=F32
        ).astype(BF16)

        @pl.when(local == 0)
        def _():
            gather_ref[:, 0:slots] = rank
            gather_ref[:, 2 * slots : 2 * slots + LANES] = chunk_ref[...].astype(BF16)

        @pl.when(local == 1)
        def _():
            gather_ref[:, slots : 2 * slots] = rank

    part = lax.dot_general(
        weight_ref[0], held[...], (((0,), (1,)), ((), ())), preferred_element_type=F32
    ).astype(BF16)
    part_ref[...] = part.reshape(part_ref.shape)


def shards(
    cotangent,
    routed_expert_index,
    chosen_gate_weight,
    routed_down_weight,
    routed_adapter_input_map,
    routed_adapter_output_map,
    routed_gate_saved,
    routed_up_saved,
    shared_down_weight,
    shared_adapter_input_map,
    shared_adapter_output_map,
    shared_gate_saved,
    shared_up_saved,
):
    n_tensor = lax.axis_size("tensor")
    group_count = lax.axis_size("expert") * lax.axis_size("dp")
    expert_local, expert_hidden, width = routed_down_weight.shape
    hidden_local = expert_hidden // n_tensor
    slot_count = routed_gate_saved.shape[2]
    rank_size = routed_adapter_output_map.shape[1]
    scale = ADAPTER_SCALE / group_count
    contract_trailing = (((1,), (1,)), ((), ()))
    contract_first = (((0,), (0,)), ((), ()))

    token_rows = lax.all_gather(cotangent, "tensor", axis=1, tiled=True)[0]
    tokens = token_rows.shape[0]

    routed_hidden, routed_gate_factor, routed_activated = swiglu_parts(
        routed_gate_saved, routed_up_saved
    )
    shared_hidden, shared_gate_factor, shared_activated = swiglu_parts(
        shared_gate_saved[0], shared_up_saved[0]
    )
    routed_inner_part = jnp.einsum(
        "fes,efr->ers", routed_hidden, routed_adapter_input_map, preferred_element_type=F32
    ).astype(BF16)
    shared_inner_part = lax.dot_general(
        shared_adapter_input_map,
        shared_hidden,
        (((0,), (1,)), ((), ())),
        preferred_element_type=F32,
    ).astype(BF16)
    packed = pl.pallas_call(
        pack_kernel,
        out_shape=jax.ShapeDtypeStruct((8 * n_tensor, PACKED), BF16),
        in_specs=whole(3),
        out_specs=whole(1)[0],
        name="pack",
    )(cotangent[0], routed_inner_part, shared_inner_part)
    packed = lax.all_to_all(packed, "tensor", split_axis=0, concat_axis=0, tiled=True)

    outgoing, own_columns, inner_chunk = pl.pallas_call(
        dispatch_kernel,
        out_shape=(
            jax.ShapeDtypeStruct((group_count * 24, width), BF16),
            jax.ShapeDtypeStruct((tokens, width), BF16),
            jax.ShapeDtypeStruct((rank_size, LANES), F32),
        ),
        in_specs=whole(3),
        out_specs=tuple(whole(3)),
        name="dispatch",
        compiler_params=pltpu.CompilerParams(vmem_limit_bytes=32 * 1024 * 1024),
    )(routed_expert_index[0].T, chosen_gate_weight[0].T, packed)
    arrived = lax.all_to_all(
        outgoing.reshape(group_count, 24, width),
        ("expert", "dp"),
        split_axis=0,
        concat_axis=0,
        tiled=True,
    ).reshape(group_count * 24, width)

    steps = 4
    fan = n_tensor // steps
    part, routed_rows, rank_part = pl.pallas_call(
        routed_kernel,
        grid=(expert_local, steps),
        out_shape=(
            jax.ShapeDtypeStruct((n_tensor, expert_local, hidden_local, slot_count), BF16),
            jax.ShapeDtypeStruct((expert_local, slot_count, width), BF16),
            jax.ShapeDtypeStruct((rank_size, expert_local * slot_count + LANES), BF16),
        ),
        in_specs=[
            pl.BlockSpec((group_count * 24, width), lambda e, j: (0, 0)),
            pl.BlockSpec((1, width, expert_hidden // steps), lambda e, j: (e, 0, j)),
            pl.BlockSpec((1, rank_size, width), lambda e, j: (e, 0, 0)),
            pl.BlockSpec((rank_size, LANES), lambda e, j: (0, 0)),
        ],
        out_specs=(
            pl.BlockSpec((fan, 1, hidden_local, slot_count), lambda e, j: (j, e, 0, 0)),
            pl.BlockSpec((1, slot_count, width), lambda e, j: (e, 0, 0)),
            pl.BlockSpec((rank_size, expert_local * slot_count + LANES), lambda e, j: (0, 0)),
        ),
        scratch_shapes=[pltpu.VMEM((slot_count, width), BF16)],
        name="routed",
        compiler_params=pltpu.CompilerParams(vmem_limit_bytes=48 * 1024 * 1024),
    )(
        arrived,
        jnp.swapaxes(routed_down_weight, 1, 2),
        routed_adapter_output_map,
        inner_chunk,
    )
    part, rank_part, token_rows = lax.optimization_barrier((part, rank_part, token_rows))
    hidden_gradient = lax.psum_scatter(
        part.reshape(n_tensor * expert_local * hidden_local, slot_count),
        "tensor",
        scatter_dimension=0,
        tiled=True,
    ).reshape(expert_local, hidden_local, slot_count)

    gathered = lax.all_gather(rank_part, "tensor", axis=0, tiled=True).reshape(
        n_tensor, rank_size, -1
    )
    edge = expert_local * slot_count
    routed_rank = jnp.sum(gathered[:, :, :edge].astype(F32), axis=0).astype(BF16)
    routed_rank = jnp.swapaxes(routed_rank.reshape(rank_size, expert_local, slot_count), 0, 1)
    inner_chunks = gathered[:, :, edge:]
    n_chunks = edge // LANES
    routed_inner = (
        inner_chunks[:n_chunks]
        .reshape(expert_local, n_chunks // expert_local, rank_size, LANES)
        .transpose(0, 2, 1, 3)
        .reshape(expert_local, rank_size, slot_count)
    )
    shared_inner = inner_chunks[n_chunks]

    shared_rank = lax.dot_general(
        token_rows, shared_adapter_output_map, contract_trailing, preferred_element_type=F32
    ).astype(BF16)
    adapter_a = lax.dot_general(
        shared_rank, shared_hidden, contract_first, preferred_element_type=F32
    )
    adapter_b = jnp.dot(shared_inner, own_columns, preferred_element_type=F32)
    adapter = jnp.concatenate([adapter_a, adapter_b], axis=1)
    adapter = jnp.sum(lax.all_gather(adapter, "dp"), axis=0)
    adapter = scale * jnp.sum(lax.all_gather(adapter, "expert"), axis=0)
    grad_a_shared = adapter[:, : adapter_a.shape[1]].T
    grad_b_shared = adapter[:, adapter_a.shape[1] :]

    shared_gradient = lax.dot_general(
        token_rows, shared_down_weight, contract_trailing, preferred_element_type=F32
    )
    shared_gradient = shared_gradient + ADAPTER_SCALE * lax.dot_general(
        shared_rank, shared_adapter_input_map, contract_trailing, preferred_element_type=F32
    )
    grad_gate_shared = (shared_gradient * shared_gate_factor).astype(BF16)[None]
    grad_up_shared = (shared_gradient * shared_activated).astype(BF16)[None]

    grad_a_routed = scale * jnp.einsum(
        "fes,ers->efr", routed_hidden, routed_rank, preferred_element_type=F32
    )
    grad_b_routed = scale * jnp.einsum(
        "ers,esd->erd", routed_inner, routed_rows, preferred_element_type=F32
    )
    low_rank = ADAPTER_SCALE * jnp.einsum(
        "ers,efr->efs", routed_rank, routed_adapter_input_map, preferred_element_type=F32
    )
    hidden_gradient = jnp.swapaxes(hidden_gradient.astype(F32) + low_rank, 0, 1)
    grad_gate_routed = (hidden_gradient * routed_gate_factor).astype(BF16)
    grad_up_routed = (hidden_gradient * routed_activated).astype(BF16)
    return (
        grad_gate_routed,
        grad_up_routed,
        grad_gate_shared,
        grad_up_shared,
        grad_a_routed,
        grad_b_routed,
        grad_a_shared,
        grad_b_shared,
    )


def solution(mesh):
    placed = (
        P(("expert", "dp"), "tensor", None),
        P(("expert", "dp"), None, None),
        P(("expert", "dp"), None, None),
        P(("expert", "dp"), None, "tensor"),
        P(("expert", "dp"), "tensor", None),
        P(("expert", "dp"), None, "tensor"),
        P("tensor", ("expert", "dp"), None),
        P("tensor", ("expert", "dp"), None),
        P("tensor", None),
        P("tensor", None),
        P(),
        P(("expert", "dp"), None, "tensor"),
        P(("expert", "dp"), None, "tensor"),
    )
    return jax.shard_map(
        shards,
        mesh=mesh,
        in_specs=placed,
        out_specs=(
            P("tensor", ("expert", "dp"), None),
            P("tensor", ("expert", "dp"), None),
            P(("expert", "dp"), None, "tensor"),
            P(("expert", "dp"), None, "tensor"),
            P(("expert", "dp"), "tensor", None),
            P(("expert", "dp"), None, "tensor"),
            P("tensor", None),
            P(None, "tensor"),
        ),
        check_vma=False,
    )
```

time: 559 us -> 211 us (0.38)
  waiting for transfers between devices: 199 us -> 12.5 us
  blocking collectives: 253 us -> 129 us
  local copies, waits for them, and re-layouts: 27.4 us -> 8.08 us
  other arithmetic: 20.3 us -> 4.89 us
  Pallas kernels: 0 us -> 9.42 us
  matrix products: 19.7 us -> 12.2 us
    psum x1 -> x0, blocking collectives: 253 us -> none  [shards(): adapter_a, adapter_b = lax.psum((adapter_a, adapter_b), ('expert', 'dp'))]
    psum x1 -> x0, waiting for transfers between devices: 110 us -> none  [shards(): lax.psum(routed_rank_part.astype(jnp.bfloat16), 'tensor')]
    all_gather x0 -> x3, blocking collectives: none -> 75.8 us  [the longest x1 37.7 us: shards(): adapter = scale * jnp.sum(lax.all_gather(adapter, 'expert'), axis=0)]
    all_gather x1, waiting for transfers between devices: 59 us -> 0.01 us  [shards(): token_rows = lax.all_gather(cotangent, 'tensor', axis=1, tiled=True)[0]]
    all_to_all x0 -> x1, blocking collectives: none -> 53.4 us  [shards(): lax.all_to_all(outgoing.reshape(group_count, 24, width), ('expert', 'dp')...]
    all_to_all x1, waiting for transfers between devices: 30 us -> 11.8 us  [shards(): lax.all_to_all(packed, 'tensor', split_axis=0, concat_axis=0, tiled=True)]
    convert_element_type x2 -> x0, local copies, waits for them, and re-layouts: 10.4 us -> none  [the longest x1 8.73 us: shards(): hidden_gradient = lax.psum_scatter(jnp.einsum('efd,esd->fes', routed_down...]
    pallas_call x0 -> x3, Pallas kernels: none -> 9.42 us  [the longest x1 6.98 us: shards(): pl.pallas_call(routed_kernel, grid=(expert_local, steps), out_shape=(jax....]
  transfers between devices with their start and end apart: 4 -> 3, of which waited for: 3 -> 1; matrix products, arithmetic and copies ran while one was open for 8% -> 7% of each run, Pallas kernels for 0% -> 4%
where the time goes in v1:
time: 211 us; the launch traced here: 210 us
  blocking collectives  129 us (61%)
  starting transfers between devices  19.5 us (9%)
  between operations  14.2 us (7%)
  waiting for transfers between devices  12.5 us (6%)
  matrix products  12.2 us (6%)
  Pallas kernels  9.42 us (4%)
  local copies, waits for them, and re-layouts  8.08 us (4%)
  other arithmetic  4.89 us (2%)
    all_to_all x1, blocking collectives, shards(): lax.all_to_all(outgoing.reshape(group_count, 24, width), ('expert', 'dp')...  53.4 us
    all_gather x1, blocking collectives, shards(): adapter = scale * jnp.sum(lax.all_gather(adapter, 'expert'), axis=0)  37.7 us
    all_gather x1, blocking collectives, shards(): lax.all_gather(rank_part, 'tensor', axis=0, tiled=True)  27.1 us
    all_to_all x1, starting transfers between devices, shards(): lax.all_to_all(packed, 'tensor', split_axis=0, concat_axis=0, tiled=True)  19.4 us
    all_to_all x1, waiting for transfers between devices, shards(): lax.all_to_all(packed, 'tensor', split_axis=0, concat_axis=0, tiled=True)  11.8 us
    all_gather x1, blocking collectives, shards(): adapter = jnp.sum(lax.all_gather(adapter, 'dp'), axis=0)  11 us
    pallas_call x1, Pallas kernels, shards(): pl.pallas_call(routed_kernel, grid=(expert_local, steps), out_shape=(jax....  6.98 us
    unnamed x36, local copies, waits for them, and re-layouts  4.77 us
  transfers between devices with their start and end apart: 3, of which 1 were waited for; matrix products, arithmetic and copies ran while one was open for 7% of the time, Pallas kernels for 4%

profile of v1, /device:TPU:1, one launch (start us, length us, event | category | flops | bytes accessed | tf_op | source)
XLA Modules:
  0.0 210.0 jit_solution(16668339928286404163)
XLA Ops:
  7.2 0.0 copy-start
  7.2 0.0 copy-start.4
  7.2 0.0 copy-start.5
  7.2 1.3 fusion.6
  8.5 0.0 copy-start.7
  8.5 0.7 copy-done.7
  9.2 1.5 fusion.4.routed_ref
  10.6 0.8 fusion.14
  11.4 0.0 copy-start.9
  11.4 0.6 copy-done.9
  12.1 1.4 fusion.5.shared_ref
  13.5 1.7 pack.1
  15.2 19.4 %all-to-all-start = ((bf16[16,8,768]{2,1,0:T(8,128)(2,1)}), bf16[16,8,768]{2,1,0:T(8,128)(2,1)S(1)}, u32[]{:S(2)}, u32[]{:S(2)}) async-start(bf16[16,8,768]{2,1,0:T(8,128)(2,1)} %bitcast.93), calls=%async_computation | async-start | bytes 393216 | tf_op jit(solution)/shard_map/all_to_all | solution.py:196
  34.6 0.0 all-gather.4.cloned.1.call-start
  34.6 0.7 all-gather.4.cloned.1.call-update
  35.3 0.0 reduce-scatter.2.cloned.1.call-start
  35.4 11.8 %all-to-all-done = bf16[16,8,768]{2,1,0:T(8,128)(2,1)S(1)} async-done(((bf16[16,8,768]{2,1,0:T(8,128)(2,1)}), bf16[16,8,768]{2,1,0:T(8,128)(2,1)S(1)}, u32[]{:S(2)}, u32[]{:S(2)}) %all-to-all-start) | async-done | bytes 196640 | tf_op jit(solution)/shard_map/all_to_all | solution.py:196
  47.2 0.0 copy-done.4
  47.2 0.7 dispatch.1
  47.9 53.4 %all_to_all.16 = bf16[64,24,448]{2,1,0:T(8,128)(2,1)S(1)} all-to-all(bf16[64,24,448]{2,1,0:T(8,128)(2,1)S(1)} %bitcast.82), channel_id=1, replica_groups=mesh['expert'=16,'tensor'=16,'dp'=4] {'expert','dp'}, dimensions={0} | all-to-all | bytes 2752512 | tf_op jit(solution)/shard_map/all_to_all | solution.py:210
  101.4 0.8 copy-done.3
  102.1 7.0 %routed.1 = (bf16[16,2,64,768]{3,2,1,0:T(8,128)(2,1)}, bf16[2,768,448]{2,1,0:T(8,128)(2,1)S(1)}, bf16[16,1664]{1,0:T(8,128)(2,1)S(1)}) custom-call(bf16[1536,448]{1,0:T(8,128)(2,1)S(1)} %bitcast.80, bf16[2,448,1024]{2,1,0:T(8,128)(2,1)S(1)} %bitcast.81, bf16[2,16,448]{2,1,0:T(8,128)(2,1)S(1)} %copy-done.3, f32[16,128]{1,0:T(8,128)S(1)} %get-tuple-element.18.chunk_ref), custom_call_target="tpu_custom_call" | custom-call | tf_op jit(solution)/shard_map/routed/pallas_call | solution.py:220
  109.1 0.6 copy-done.2
  109.7 0.0 reduce-scatter.2.cloned.1.call-update
  109.7 27.1 %all_gather.19 = bf16[256,1664]{1,0:T(8,128)(2,1)S(1)} all-gather(bf16[16,1664]{1,0:T(8,128)(2,1)} %copy-done.2), channel_id=1, replica_groups=mesh['expert'=16,'tensor'=16,'dp'=4] {'tensor'}, dimensions={0}, use_global_device_ids=true | all-gather | bytes 905216 | tf_op jit(solution)/shard_map/all_gather | solution.py:256
  136.9 0.7 slice.24
  137.5 0.3 copy-done.6
  137.8 0.7 slice_reduce_fusion
  138.6 1.4 reshape.50
  140.0 2.1 convolution_convert_fusion.1
  142.1 0.1 fusion.30
  142.2 0.8 fusion.28
  143.0 11.0 %all-gather = f32[64,576]{1,0:T(8,128)} all-gather(f32[16,576]{1,0:T(8,128)S(1)} %pad_maximum_fusion), channel_id=2, replica_groups=mesh['expert'=16,'tensor'=16,'dp'=4] {'dp'}, dimensions={0}, use_global_device_ids=true | all-gather | bytes 184320 | tf_op jit(solution)/shard_map/all_gather | solution.py:280
  154.0 0.9 reduce_sum.31
  155.0 37.7 %all-gather.1 = f32[256,576]{1,0:T(8,128)} all-gather(f32[16,576]{1,0:T(8,128)S(1)} %reduce_sum.31), channel_id=3, replica_groups=mesh['expert'=16,'tensor'=16,'dp'=4] {'expert'}, dimensions={0}, use_global_device_ids=true | all-gather | bytes 626688 | tf_op jit(solution)/shard_map/all_gather | solution.py:281
  192.7 1.1 reduce_sum.32
  193.8 0.6 slice.27
  194.4 0.0 copy-start.8
  194.4 0.0 copy-start.12
  194.5 2.2 %fusion.29 = f32[128,128]{1,0:T(8,128)S(1)} fusion(bf16[128,7168]{1,0:T(8,128)(2,1)} %bitcast.87, bf16[128,7168]{1,0:T(8,128)(2,1)S(1)} %copy-done), kind=kOutput, calls=%fused_computation.53 | convolution fusion | flops 234881024 | bytes 3735552 | tf_op jit(solution)/shard_map/dot_general | solution.py:285
  196.7 0.0 copy-start.15
  196.7 0.8 fusion.26
  197.5 0.6 slice_bitcast_fusion
  198.1 0.8 convolution_multiply_fusion.3
  198.9 0.9 convolution_multiply_fusion.1
  199.9 1.5 multiply_convert_fusion
  201.4 0.9 copy.48
  202.2 0.9 copy.49
  (24 shorter events, 0.1 us)
Async XLA Ops:
  7.2 187.3 %copy-start = (bf16[128,7168]{1,0:T(8,128)(2,1)S(1)}, bf16[128,7168]{1,0:T(8,128)(2,1)}, u32[]{:S(2)}) copy-start(bf16[128,7168]{1,0:T(8,128)(2,1)} %param.21) | copy-start | bytes 5505028
  7.2 40.0 %copy-start.4 = (s32[1,128,8]{1,2,0:T(8,128)S(1)}, s32[1,128,8]{1,2,0:T(8,128)}, u32[]{:S(2)}) copy-start(s32[1,128,8]{1,2,0:T(8,128)} %param.14) | copy-start | bytes 12292
  7.2 40.0 %copy-start.5 = (f32[1,128,8]{1,2,0:T(8,128)S(1)}, f32[1,128,8]{1,2,0:T(8,128)}, u32[]{:S(2)}) copy-start(f32[1,128,8]{1,2,0:T(8,128)} %param.15) | copy-start | bytes 12292
  8.5 0.7 copy-start.7
  11.4 0.6 copy-start.9
  15.2 32.0 %all-to-all-start = ((bf16[16,8,768]{2,1,0:T(8,128)(2,1)}), bf16[16,8,768]{2,1,0:T(8,128)(2,1)S(1)}, u32[]{:S(2)}, u32[]{:S(2)}) async-start(bf16[16,8,768]{2,1,0:T(8,128)(2,1)} %bitcast.93), calls=%async_computation | async-start | bytes 393216 | tf_op jit(solution)/shard_map/all_to_all | solution.py:196
  34.6 75.1 %all-gather.4.cloned.1.call-start = ((), (), s32[]{:S(2)}) async-start(), calls=%async_computation.3 | async-start | bytes 1949696 | tf_op jit(solution)/shard_map/all_gather | solution.py:171
  35.3 164.5 %reduce-scatter.2.cloned.1.call-start = ((), (), s32[]{:S(2)}) async-start(), calls=%async_computation.4 | async-start | bytes 3342336 | tf_op jit(solution)/shard_map/reduce_scatter | solution.py:249
  47.2 54.2 %copy-start.1 = (bf16[2,1024,448]{1,2,0:T(8,128)(2,1)S(1)}, bf16[2,1024,448]{1,2,0:T(8,128)(2,1)}, u32[]{:S(2)}) copy-start(bf16[2,1024,448]{1,2,0:T(8,128)(2,1)} %param.16) | copy-start | bytes 5505028
  101.4 0.8 copy-start.3
  109.1 0.6 copy-start.2
  136.9 1.0 copy-start.6
  140.0 2.1 copy-start.10
  194.4 2.3 %copy-start.13 = (bf16[1,128,128]{2,1,0:T(8,128)(2,1)S(1)}, bf16[1,128,128]{2,1,0:T(8,128)(2,1)}, u32[]{:S(2)}) copy-start(bf16[1,128,128]{2,1,0:T(8,128)(2,1)} %param.25) | copy-start | bytes 98308
  194.4 2.3 %copy-start.14 = (bf16[1,128,128]{2,1,0:T(8,128)(2,1)S(1)}, bf16[1,128,128]{2,1,0:T(8,128)(2,1)}, u32[]{:S(2)}) copy-start(bf16[1,128,128]{2,1,0:T(8,128)(2,1)} %param.24) | copy-start | bytes 98308
  194.4 2.3 %copy-start.16 = (bf16[128,16]{0,1:T(8,128)(2,1)S(1)}, bf16[128,16]{0,1:T(8,128)(2,1)}, u32[]{:S(2)}) copy-start(bf16[128,16]{0,1:T(8,128)(2,1)} %param.22) | copy-start | bytes 12292
  194.4 3.7 %copy-start.8 = (bf16[64,2,768]{2,0,1:T(8,128)(2,1)S(1)}, bf16[64,2,768]{2,0,1:T(8,128)(2,1)}, u32[]{:S(2)}) copy-start(bf16[64,2,768]{2,0,1:T(8,128)(2,1)} %copy-done.7) | copy-start | bytes 589828
  194.4 3.7 %copy-start.12 = (bf16[16,2,768]{2,1,0:T(2,128)(2,1)S(1)}, bf16[16,2,768]{2,1,0:T(2,128)(2,1)}, u32[]{:S(2)}) copy-start(bf16[16,2,768]{2,1,0:T(2,128)(2,1)} %reshape.50) | copy-start | bytes 147460
  194.5 4.5 %copy-start.11 = (bf16[12,16,128]{2,1,0:T(8,128)(2,1)S(1)}, bf16[12,16,128]{2,1,0:T(8,128)(2,1)}, u32[]{:S(2)}) copy-start(bf16[12,16,128]{2,1,0:T(8,128)(2,1)} %slice.24) | copy-start | bytes 147460
  196.7 3.2 %copy-start.15 = (bf16[2,64,16]{1,2,0:T(8,128)(2,1)S(1)}, bf16[2,64,16]{1,2,0:T(8,128)(2,1)}, u32[]{:S(2)}) copy-start(bf16[2,64,16]{1,2,0:T(8,128)(2,1)} %param.17) | copy-start | bytes 12292
Sparse Core Ops, SparseCore 0:
  38.1 69.1 all-gather.3
  110.8 76.9 reduce-scatter.1
